TPU v7x, 32 devices: a whole 2x2x4 slice. The times are simulated.
32 devices in a mesh: dp: 8 (over y, x, core), expert: 4 (over z).
Axes of the slice: x: 2, y: 2, z: 4, core: 2. Of those that a mesh axis runs over, the one named last changes fastest.
Arguments:
- residual: bfloat16 [4096, 2048], P(('dp', 'expert')), may hold values from -6 to 6
- grad_stream: bfloat16 [4096, 2048], P(('dp', 'expert')), may hold values from -6 to 6
- expert_gain: float32 [2048], replicated, may hold values from 0.5 to 1.5
- router_weight: bfloat16 [2048, 32], replicated, may hold values from -0.125 to 0.125
- gate_up_weight: bfloat16 [32, 2048, 1536], P('expert', 'dp'), may hold values from -0.125 to 0.125
- down_weight: bfloat16 [32, 2048, 768], P('expert', 'dp'), may hold values from -0.21875 to 0.21875
- need_lists: int32 [4, 2], replicated, may hold values from 0 to 31, as said below
- routes: int32 [4096, 1], P(('dp', 'expert')), may hold values from 0 to 1
Outputs:
- stream: bfloat16 [4096, 2048], P(('dp', 'expert'))
- grad_residual: bfloat16 [4096, 2048], P(('dp', 'expert'))
Inputs may be any that keep to these rules, and one draw needn't show every extreme that they name: `need_lists`: row c lists 2 experts with different owner indices (expert id // 8).
All inputs are finite; a program needn't handle non-finite values.
Results may differ from a plain program's by a relative error of at most 0.008.
Values may be sent and summed in bfloat16 or wider, within the bound.
A program may use at most 128 MiB of HBM per device.

v0:
```python
import jax
import jax.numpy as jnp
from jax import lax
from jax.sharding import PartitionSpec as P

eps = 1e-05


def partner(value, axis, stride):
    mask = 2**stride
    pairs = [(source, source ^ mask) for source in range(lax.axis_size(axis))]
    return lax.ppermute(value, axis, pairs)


def norm_factor(values):
    return lax.rsqrt(jnp.mean(values * values, axis=-1, keepdims=True) + eps)


def norm_backward(values, factor, gain, grad):
    scaled = gain * grad
    return factor * scaled - values * factor**3 * jnp.mean(values * scaled, axis=-1, keepdims=True)


def body(
    residual,
    grad_stream,
    expert_gain,
    router_weight,
    gate_up_weight,
    down_weight,
    need_lists,
    routes,
):
    column = lax.axis_index("expert")
    ranks = lax.axis_size("dp")
    parity = lax.axis_index("dp") % 2
    held = gate_up_weight.shape[0]
    width = down_weight.shape[2]
    tokens = residual.shape[0]
    listed = lax.dynamic_index_in_dim(need_lists, column, 0, keepdims=False)
    owner_of = need_lists // held
    local_of = need_lists % held
    mine = owner_of == column
    has_one = jnp.any(mine, axis=1)
    local_pick = jnp.sum(jnp.where(mine, local_of, 0), axis=1)
    owned = jnp.stack(
        [gate_up_weight[:, :, :width], gate_up_weight[:, :, width:], down_weight], axis=2
    )
    outgoing = jnp.where(
        has_one[:, None, None, None],
        jnp.take(owned, local_pick, axis=0),
        jnp.zeros((), jnp.bfloat16),
    )
    arrived = lax.all_to_all(outgoing, "expert", split_axis=0, concat_axis=0, tiled=True)
    slot_rows = jnp.take(arrived, listed // held, axis=0)
    spread_out = jnp.broadcast_to(slot_rows[None], (ranks // 2,) + slot_rows.shape).reshape(
        (ranks,) + slot_rows.shape[1:]
    )
    stream_in = residual.astype(jnp.float32)
    factor_in = norm_factor(stream_in)
    normed = (stream_in * factor_in * expert_gain).astype(jnp.bfloat16)
    router_cols = jnp.take(router_weight, listed, axis=1)
    logits = jnp.dot(normed, router_cols, preferred_element_type=jnp.float32)
    gates = jax.nn.sigmoid(logits - logits[:, ::-1])
    select = (routes == jnp.arange(2, dtype=jnp.int32)[None, :]).astype(jnp.float32)
    mix = gates * select
    mix_here = lax.dynamic_index_in_dim(mix, parity, 1, keepdims=False)
    mix_there = lax.dynamic_index_in_dim(mix, 1 - parity, 1, keepdims=False)
    grad_out = grad_stream.astype(jnp.float32)
    send_grad = (mix_there[:, None] * grad_out).astype(jnp.bfloat16)
    partner_normed, partner_grad = partner((normed, send_grad), "dp", 0)
    pair_normed = jnp.concatenate([normed, partner_normed], axis=0)
    weights = lax.all_to_all(spread_out, "dp", split_axis=0, concat_axis=1, tiled=True)[0]
    hidden = jnp.einsum(
        "td,dkf->tkf", pair_normed, weights[:, :2], preferred_element_type=jnp.float32
    )
    gate_part = hidden[:, 0]
    up_part = hidden[:, 1]
    sigma = jax.nn.sigmoid(gate_part)
    silu_gate = gate_part * sigma
    act = (silu_gate * up_part).astype(jnp.bfloat16)
    branch = jnp.einsum("tf,df->td", act, weights[:, 2], preferred_element_type=jnp.float32).astype(
        jnp.bfloat16
    )
    other_branch = partner(branch[tokens:], "dp", 0)
    branch_here = branch[:tokens].astype(jnp.float32)
    branch_there = other_branch.astype(jnp.float32)
    stream = (
        stream_in + mix_here[:, None] * branch_here + mix_there[:, None] * branch_there
    ).astype(jnp.bfloat16)
    mix_grad_here = jnp.sum(branch_here * grad_out, axis=-1)
    mix_grad_there = jnp.sum(branch_there * grad_out, axis=-1)
    grad_mix = jnp.where(
        parity == 0,
        jnp.stack([mix_grad_here, mix_grad_there], axis=1),
        jnp.stack([mix_grad_there, mix_grad_here], axis=1),
    )
    grad_branch = jnp.concatenate(
        [(mix_here[:, None] * grad_out).astype(jnp.bfloat16), partner_grad], axis=0
    )
    grad_act = jnp.einsum(
        "td,df->tf", grad_branch, weights[:, 2], preferred_element_type=jnp.float32
    )
    slope = sigma * (1.0 + gate_part * (1.0 - sigma))
    grad_hidden = jnp.stack([grad_act * up_part * slope, grad_act * silu_gate], axis=1).astype(
        jnp.bfloat16
    )
    expert_term = jnp.einsum(
        "tkf,dkf->td", grad_hidden, weights[:, :2], preferred_element_type=jnp.float32
    ).astype(jnp.bfloat16)
    other_term = partner(expert_term[tokens:], "dp", 0)
    grad_gates = grad_mix * select
    grad_logits = (
        gates * (grad_gates - jnp.sum(gates * grad_gates, axis=-1, keepdims=True))
    ).astype(jnp.bfloat16)
    grad_normed = expert_term[:tokens].astype(jnp.float32) + other_term.astype(jnp.float32)
    grad_normed = grad_normed + jnp.einsum(
        "tn,dn->td", grad_logits, router_cols, preferred_element_type=jnp.float32
    )
    grad_residual = (
        grad_out + norm_backward(stream_in, factor_in, expert_gain, grad_normed)
    ).astype(jnp.bfloat16)
    return (stream, grad_residual)


def solution(mesh):
    return jax.shard_map(
        body,
        mesh=mesh,
        in_specs=(
            P(("dp", "expert"), None),
            P(("dp", "expert"), None),
            P(),
            P(),
            P("expert", "dp", None),
            P("expert", "dp", None),
            P(),
            P(("dp", "expert"), None),
        ),
        out_specs=(P(("dp", "expert"), None), P(("dp", "expert"), None)),
        check_vma=False,
    )
```

profile of v0, /device:TPU:0, one launch (start us, length us, event | category | flops | bytes accessed | tf_op | source)
XLA Modules:
  0.0 289.3 jit_solution(1580183164395549183)
XLA Ops:
  0.6 0.0 copy-start
  0.6 0.7 fusion.64
  1.4 0.7 fusion.49
  2.1 5.0 %slice_bitcast_fusion.2 = (bf16[8,256,1,768]{3,1,0,2:T(8,128)(2,1)S(1)}, bf16[8,256,1,768]{3,1,0,2:T(8,128)(2,1)}) fusion(bf16[8,256,1536]{2,1,0:T(8,128)(2,1)} %param.12), kind=kLoop, calls=%fused_computation.11 | loop fusion | bytes 12582912 | tf_op jit(solution)/shard_map/stack | solution.py:46
  7.1 7.0 %pad_maximum_fusion = bf16[8,256,3,768]{3,1,0,2:T(8,128)(2,1)} fusion(bf16[8,256,1,768]{3,1,0,2:T(8,128)(2,1)} %bitcast.97, bf16[8,256,1,768]{3,1,0,2:T(8,128)(2,1)} %get-tuple-element.9, bf16[8,256,1,768]{3,1,0,2:T(8,128)(2,1)S(1)} %get-tuple-element.8), kind=kLoop, calls=%fused_computation.3 | loop fusion | flops 9437184 | bytes 18874368 | tf_op jit(solution)/shard_map/stack | solution.py:46
  14.1 6.8 %gather_fusion.1 = bf16[4,256,3,768]{3,1,2,0:T(8,128)(2,1)} fusion(bf16[8,256,3,768]{3,1,0,2:T(8,128)(2,1)} %pad_maximum_fusion, s32[1024]{0:T(1024)S(1)} %pad_clamp_fusion.1), kind=kCustom, calls=%fused_computation.1 | custom fusion | bytes 9437200 | tf_op jit(solution)/shard_map/jit(_take)/gather | solution.py:51
  20.8 5.2 %select_select_fusion = bf16[4,256,3,768]{3,1,2,0:T(8,128)(2,1)} fusion(bf16[4,256,3,768]{3,1,2,0:T(8,128)(2,1)} %gather_fusion.1, pred[4]{0:T(512)(128)(4,1)S(1)} %compare_and_fusion, pred[4]{0:T(512)(128)(4,1)S(1)} %get-tuple-element.6), kind=kLoop, calls=%fused_computation.8 | loop fusion | flops 4718592 | bytes 9437192 | tf_op jit(solution)/shard_map/jit(_where)/select_n | solution.py:49
  26.0 0.0 copy-start.5
  26.0 6.4 %all-to-all-start = ((bf16[4,256,3,768]{3,1,2,0:T(8,128)(2,1)}), bf16[4,256,3,768]{3,1,2,0:T(8,128)(2,1)}, u32[]{:S(2)}, u32[]{:S(2)}) async-start(bf16[4,256,3,768]{3,1,2,0:T(8,128)(2,1)} %select_select_fusion), calls=%async_computation | async-start | bytes 9437184 | tf_op jit(solution)/shard_map/all_to_all | solution.py:54
  32.5 0.0 copy-done.5
  32.5 0.2 dynamic-slice_reduce_fusion
  32.7 104.5 %all-to-all-done = bf16[4,256,3,768]{3,1,2,0:T(8,128)(2,1)} async-done(((bf16[4,256,3,768]{3,1,2,0:T(8,128)(2,1)}), bf16[4,256,3,768]{3,1,2,0:T(8,128)(2,1)}, u32[]{:S(2)}, u32[]{:S(2)}) %all-to-all-start) | async-done | bytes 4718624 | tf_op jit(solution)/shard_map/all_to_all | solution.py:54
  137.2 3.0 %gather_fusion.2 = bf16[2,256,3,768]{3,1,2,0:T(8,128)(2,1)S(1)} fusion(bf16[4,256,3,768]{3,1,2,0:T(8,128)(2,1)} %all-to-all-done, s32[1024]{0:T(1024)S(1)} %pad_clamp_fusion), kind=kCustom, calls=%fused_computation.2 | custom fusion | bytes 4718600 | tf_op jit(solution)/shard_map/jit(_take)/gather | solution.py:55
  140.3 0.3 broadcast_select_fusion
  140.6 4.7 %broadcast_in_dim.69 = bf16[4,2,256,3,768]{4,2,3,1,0:T(8,128)(2,1)} broadcast(bf16[2,256,3,768]{3,1,2,0:T(8,128)(2,1)S(1)} %broadcast_select_fusion), dimensions={1,2,3,4} | broadcast | bytes 11796480 | tf_op jit(solution)/shard_map/broadcast_in_dim | solution.py:56
  145.3 0.0 copy-start.1
  145.3 0.0 copy-start.4
  145.3 5.2 %all-to-all-start.1 = ((bf16[8,256,3,768]{3,1,2,0:T(8,128)(2,1)}), bf16[8,256,3,768]{3,1,2,0:T(8,128)(2,1)}, u32[]{:S(2)}, u32[]{:S(2)}) async-start(bf16[8,256,3,768]{3,1,2,0:T(8,128)(2,1)} %bitcast.92), calls=%async_computation.1 | async-start | bytes 18874368 | tf_op jit(solution)/shard_map/all_to_all | solution.py:73
  150.5 0.0 copy-done.1
  150.5 0.2 fusion.15
  150.7 0.0 copy-done.4
  150.7 0.2 fusion.17
  150.9 0.0 copy-start.3
  150.9 0.4 collective-permute-start
  151.3 104.4 %all-to-all-done.1 = bf16[8,256,3,768]{3,1,2,0:T(8,128)(2,1)} async-done(((bf16[8,256,3,768]{3,1,2,0:T(8,128)(2,1)}), bf16[8,256,3,768]{3,1,2,0:T(8,128)(2,1)}, u32[]{:S(2)}, u32[]{:S(2)}) %all-to-all-start.1) | async-done | bytes 9437216 | tf_op jit(solution)/shard_map/all_to_all | solution.py:73
  255.8 8.2 %copy.11 = bf16[8,256,3,768]{3,1,0,2:T(8,128)(2,1)} copy(bf16[8,256,3,768]{3,1,2,0:T(8,128)(2,1)} %all-to-all-done.1) | data formatting | bytes 18874368 | tf_op jit(solution)/shard_map/all_to_all | solution.py:73
  264.0 0.0 collective-permute-done
  264.0 0.0 copy-done.3
  264.0 4.6 %fusion.2 = f32[256,2,768]{2,0,1:T(8,128)S(1)} fusion(bf16[2048,3,768]{2,0,1:T(8,128)(2,1)} %bitcast.93, bf16[128,2048]{1,0:T(8,128)(2,1)S(1)} %collective-permute-done, bf16[128,2048]{1,0:T(8,128)(2,1)S(1)} %fusion.17), kind=kOutput, calls=%fused_computation.6 | convolution fusion | flops 1612709888 | bytes 8912896 | tf_op jit(solution)/shard_map/td,dkf->tkf/dot_general | solution.py:74
  268.6 0.0 copy-start.7
  268.6 3.5 %fusion.12 = bf16[256,2048]{1,0:T(8,128)(2,1)S(1)} fusion(bf16[2048,3,768]{2,0,1:T(8,128)(2,1)} %bitcast.94, f32[256,2,768]{2,0,1:T(8,128)S(1)} %fusion.2), kind=kOutput, calls=%fused_computation.16 | convolution fusion | flops 807010304 | bytes 5767168 | tf_op jit(solution)/shard_map/tf,df->td/dot_general | solution.py:82
  272.1 0.0 copy-done.7
  272.1 0.0 copy-start.2
  272.1 0.0 copy-start.6
  272.2 0.1 collective-permute-start.1
  272.3 0.0 copy-done
  272.3 0.6 gather_fusion
  272.9 1.3 fusion.63
  274.2 0.0 collective-permute-done.1
  274.2 0.0 copy-done.2
  274.2 0.3 fusion.24
  274.6 0.0 copy-done.6
  274.6 0.2 fusion.21
  274.9 0.5 collective-permute-start.2
  275.4 1.5 collective-permute-done.2
  276.9 3.4 %fusion.45 = (bf16[256,1,768]{2,0,1:T(8,128)(2,1)S(1)}, bf16[256,1,768]{2,0,1:T(8,128)(2,1)S(1)}) fusion(f32[256,2,768]{2,0,1:T(8,128)} %copy-done.7, bf16[2048,3,768]{2,0,1:T(8,128)(2,1)} %bitcast.95, bf16[128,2048]{1,0:T(8,128)(2,1)S(1)} %collective-permute-done.2, bf16[128,2048]{1,0:T(8,128)(2,1)S(1)} %get-tuple-element.14), kind=kOutput, calls=%fused_computation.69 | convolution fusion | flops 809959424 | bytes 6553600 | tf_op jit(solution)/shard_map/td,df->tf/dot_general | solution.py:101
  280.4 4.6 %fusion.9 = bf16[256,2048]{1,0:T(8,128)(2,1)S(1)} fusion(bf16[2048,3,768]{2,0,1:T(8,128)(2,1)} %bitcast.96, bf16[256,1,768]{2,0,1:T(8,128)(2,1)S(1)} %get-tuple-element.11, bf16[256,1,768]{2,0,1:T(8,128)(2,1)S(1)} %get-tuple-element.10), kind=kOutput, calls=%fused_computation.15 | convolution fusion | flops 1611530240 | bytes 8126464 | tf_op jit(solution)/shard_map/tkf,dkf->td/dot_general | solution.py:108
  285.0 0.4 collective-permute-start.3
  285.5 1.5 collective-permute-done.3
  287.0 0.5 fusion.20
  287.6 1.7 fusion.25
  (15 shorter events, 0.2 us)
Async XLA Ops:
  0.6 271.6 %copy-start = (bf16[2048,32]{0,1:T(8,128)(2,1)S(1)}, bf16[2048,32]{0,1:T(8,128)(2,1)}, u32[]{:S(2)}) copy-start(bf16[2048,32]{0,1:T(8,128)(2,1)} %param.11) | copy-start | bytes 393220
  26.0 6.5 %copy-start.5 = (s32[4,2]{0,1:T(2,128)S(1)}, s32[4,2]{0,1:T(2,128)}, u32[]{:S(2)}) copy-start(s32[4,2]{0,1:T(2,128)} %param.14) | copy-start | bytes 100
  26.0 111.2 %all-to-all-start = ((bf16[4,256,3,768]{3,1,2,0:T(8,128)(2,1)}), bf16[4,256,3,768]{3,1,2,0:T(8,128)(2,1)}, u32[]{:S(2)}, u32[]{:S(2)}) async-start(bf16[4,256,3,768]{3,1,2,0:T(8,128)(2,1)} %select_select_fusion), calls=%async_computation | async-start | bytes 9437184 | tf_op jit(solution)/shard_map/all_to_all | solution.py:54
  145.3 5.2 %copy-start.1 = (bf16[128,2048]{1,0:T(8,128)(2,1)S(1)}, bf16[128,2048]{1,0:T(8,128)(2,1)}, u32[]{:S(2)}) copy-start(bf16[128,2048]{1,0:T(8,128)(2,1)} %param.8) | copy-start | bytes 1572868
  145.3 5.4 %copy-start.4 = (f32[2048]{0:T(1024)S(1)}, f32[2048]{0:T(1024)}, u32[]{:S(2)}) copy-start(f32[2048]{0:T(1024)} %param.10) | copy-start | bytes 24580
  145.3 110.5 %all-to-all-start.1 = ((bf16[8,256,3,768]{3,1,2,0:T(8,128)(2,1)}), bf16[8,256,3,768]{3,1,2,0:T(8,128)(2,1)}, u32[]{:S(2)}, u32[]{:S(2)}) async-start(bf16[8,256,3,768]{3,1,2,0:T(8,128)(2,1)} %bitcast.92), calls=%async_computation.1 | async-start | bytes 18874368 | tf_op jit(solution)/shard_map/all_to_all | solution.py:73
  150.9 113.1 %copy-start.3 = (bf16[128,2048]{1,0:T(8,128)(2,1)}, bf16[128,2048]{1,0:T(8,128)(2,1)S(1)}, u32[]{:S(2)}) copy-start(bf16[128,2048]{1,0:T(8,128)(2,1)S(1)} %fusion.17) | copy-start | bytes 1572868
  150.9 113.1 %collective-permute-start = (bf16[128,2048]{1,0:T(8,128)(2,1)S(1)}, bf16[128,2048]{1,0:T(8,128)(2,1)S(1)}, u32[]{:S(2)}, u32[]{:S(2)}) collective-permute-start(bf16[128,2048]{1,0:T(8,128)(2,1)S(1)} %fusion.17), channel_id=1, source_target_pairs={{0,4},{4,0},{8,12},{12,8},{16,20},{20,16},{24,28},{28,24},{1,5},{5... | collective-permute-start | bytes 1572872 | tf_op jit(solution)/shard_map/ppermute | solution.py:12
  268.6 3.5 %copy-start.7 = (f32[256,2,768]{2,0,1:T(8,128)}, f32[256,2,768]{2,0,1:T(8,128)S(1)}, u32[]{:S(2)}) copy-start(f32[256,2,768]{2,0,1:T(8,128)S(1)} %fusion.2) | copy-start | bytes 4718596
  272.1 2.1 copy-start.2
  272.1 2.5 copy-start.6
  272.2 2.0 collective-permute-start.1
  274.9 2.1 collective-permute-start.2
  285.0 2.0 collective-permute-start.3
where the time goes:
time: 290 us; the launch traced here: 289 us
  waiting for transfers between devices  212 us (73%)
  local copies, waits for them, and re-layouts  28.6 us (10%)
  matrix products  18 us (6%)
  other arithmetic  16.7 us (6%)
  starting transfers between devices  13.1 us (5%)
    all_to_all x1, waiting for transfers between devices, body(): lax.all_to_all(outgoing, 'expert', split_axis=0, concat_axis=0, tiled=True)  105 us
    all_to_all x1, waiting for transfers between devices, body(): lax.all_to_all(spread_out, 'dp', split_axis=0, concat_axis=1, tiled=True)[0]  104 us
    all_to_all x1, local copies, waits for them, and re-layouts, body(): lax.all_to_all(spread_out, 'dp', split_axis=0, concat_axis=1, tiled=True)[0]  8.21 us
    another operation x1, other arithmetic, body(): jnp.stack([gate_up_weight[:, :, :width], gate_up_weight[:, :, width:], do...  6.99 us
    gather x1, local copies, waits for them, and re-layouts, body(): jnp.take(owned, local_pick, axis=0)  6.77 us
    all_to_all x1, starting transfers between devices, body(): lax.all_to_all(outgoing, 'expert', split_axis=0, concat_axis=0, tiled=True)  6.45 us
  transfers between devices with their start and end apart: 6, of which 4 were waited for; matrix products, arithmetic and copies ran while one was open for 4% of the time, Pallas kernels for 0%

commit v1 on v0

--- a/solution.py
+++ b/solution.py
@@ -1,9 +1,14 @@
+import functools
+
 import jax
 import jax.numpy as jnp
 from jax import lax
+from jax.experimental import pallas as pl
+from jax.experimental.pallas import tpu as pltpu
 from jax.sharding import PartitionSpec as P
 
 eps = 1e-05
+MESH = pl.DeviceIdType.MESH
 
 
 def partner(value, axis, stride):
@@ -19,6 +24,164 @@
 def norm_backward(values, factor, gain, grad):
     scaled = gain * grad
     return factor * scaled - values * factor**3 * jnp.mean(values * scaled, axis=-1, keepdims=True)
+
+
+def pick_kernel(columns, slots, need_ref, gate_up_ref, down_ref, out_ref, sems):
+    column = lax.axis_index("expert")
+    held = gate_up_ref.shape[0]
+    joined = gate_up_ref.shape[2]
+    width = down_ref.shape[2]
+    copies = []
+    for j in range(columns):
+        pick = jnp.int32(0)
+        for s in range(slots):
+            expert = need_ref[j, s]
+            pick = jnp.where(expert // held == column, expert % held, pick)
+        copies.append(
+            pltpu.make_async_copy(
+                gate_up_ref.at[pick], out_ref.at[j, :, pl.ds(0, joined)], sems.at[j, 0]
+            )
+        )
+        copies.append(
+            pltpu.make_async_copy(
+                down_ref.at[pick], out_ref.at[j, :, pl.ds(joined, width)], sems.at[j, 1]
+            )
+        )
+    for copy in copies:
+        copy.start()
+    for copy in copies:
+        copy.wait()
+
+
+def pick(need_lists, gate_up_weight, down_weight):
+    columns, slots = need_lists.shape
+    rows = down_weight.shape[1]
+    total = gate_up_weight.shape[2] + down_weight.shape[2]
+    return pl.pallas_call(
+        functools.partial(pick_kernel, columns, slots),
+        out_shape=jax.ShapeDtypeStruct((columns, rows, total), jnp.bfloat16),
+        in_specs=[
+            pl.BlockSpec(memory_space=pltpu.SMEM),
+            pl.BlockSpec(memory_space=pl.ANY),
+            pl.BlockSpec(memory_space=pl.ANY),
+        ],
+        out_specs=pl.BlockSpec(memory_space=pl.ANY),
+        scratch_shapes=[pltpu.SemaphoreType.DMA((columns, 2))],
+    )(need_lists, gate_up_weight, down_weight)
+
+
+def move_kernel(columns, ranks, held, chunks, need_ref, out_ref, weights_ref, *scratch):
+    arrived = scratch[:chunks]
+    slots = scratch[chunks : 2 * chunks]
+    zs, zr, ps, pr, own = scratch[2 * chunks :]
+    column = lax.axis_index("expert")
+    me = lax.axis_index("dp")
+    rows = out_ref.shape[1]
+    part = rows // chunks
+    depth = 2
+
+    barrier = pltpu.get_barrier_semaphore()
+    for k in range(1, columns):
+        pl.semaphore_signal(
+            barrier, inc=1, device_id=(me, lax.rem(column + k, columns)), device_id_type=MESH
+        )
+    for k in range(1, ranks):
+        pl.semaphore_signal(
+            barrier, inc=1, device_id=(lax.rem(me + k, ranks), column), device_id_type=MESH
+        )
+    pl.semaphore_wait(barrier, columns + ranks - 2)
+
+    def own_copy(c):
+        return pltpu.make_async_copy(
+            out_ref.at[column, pl.ds(c * part, part)], arrived[c].at[column], own.at[c]
+        )
+
+    def column_copy(c, k):
+        to = lax.rem(column + k, columns)
+        return pltpu.make_async_remote_copy(
+            src_ref=out_ref.at[to, pl.ds(c * part, part)],
+            dst_ref=arrived[c].at[column],
+            send_sem=zs.at[k - 1, c],
+            recv_sem=zr.at[k - 1, c],
+            device_id=(me, to),
+            device_id_type=MESH,
+        )
+
+    place = pl.multiple_of(me * rows, rows)
+
+    def spread_copy(c, k):
+        to = lax.rem(me + k, ranks)
+        return pltpu.make_async_remote_copy(
+            src_ref=slots[c].at[lax.rem(to, 2)],
+            dst_ref=weights_ref.at[pl.ds(place + c * part, part)],
+            send_sem=ps.at[k - 1, c],
+            recv_sem=pr.at[k - 1, c],
+            device_id=(to, column),
+            device_id_type=MESH,
+        )
+
+    def keep_copy(c):
+        return pltpu.make_async_copy(
+            slots[c].at[lax.rem(me, 2)],
+            weights_ref.at[pl.ds(place + c * part, part)],
+            own.at[chunks + c],
+        )
+
+    def start_columns(c):
+        own_copy(c).start()
+        for k in range(1, columns):
+            column_copy(c, k).start()
+
+    for c in range(min(depth, chunks)):
+        start_columns(c)
+    for c in range(chunks):
+        own_copy(c).wait()
+        for k in range(1, columns):
+            column_copy(c, k).wait_recv()
+        if c + depth < chunks:
+            for k in range(1, columns):
+                column_copy(c, k).wait_send()
+            start_columns(c + depth)
+        for s in range(2):
+            owner = need_ref[column, s] // held
+            slots[c][s] = arrived[c][owner]
+        for k in range(1, ranks):
+            spread_copy(c, k).start()
+        keep_copy(c).start()
+    for c in range(max(chunks - depth, 0), chunks):
+        for k in range(1, columns):
+            column_copy(c, k).wait_send()
+    for c in range(chunks):
+        keep_copy(c).wait()
+        for k in range(1, ranks):
+            spread_copy(c, k).wait()
+
+
+def move(need_lists, outgoing, held, ranks):
+    columns, rows, total = outgoing.shape
+    chunks = max(1, min(8, rows // 32))
+    part = rows // chunks
+    return pl.pallas_call(
+        functools.partial(move_kernel, columns, ranks, held, chunks),
+        out_shape=jax.ShapeDtypeStruct((ranks * rows, total), jnp.bfloat16),
+        in_specs=[
+            pl.BlockSpec(memory_space=pltpu.SMEM),
+            pl.BlockSpec(memory_space=pl.ANY),
+        ],
+        out_specs=pl.BlockSpec(memory_space=pl.ANY),
+        scratch_shapes=[pltpu.VMEM((columns, part, total), jnp.bfloat16) for _ in range(chunks)]
+        + [pltpu.VMEM((2, part, total), jnp.bfloat16) for _ in range(chunks)]
+        + [
+            pltpu.SemaphoreType.DMA((columns - 1, chunks)),
+            pltpu.SemaphoreType.DMA((columns - 1, chunks)),
+            pltpu.SemaphoreType.DMA((ranks - 1, chunks)),
+            pltpu.SemaphoreType.DMA((ranks - 1, chunks)),
+            pltpu.SemaphoreType.DMA((2 * chunks,)),
+        ],
+        compiler_params=pltpu.CompilerParams(
+            collective_id=0, has_side_effects=True, vmem_limit_bytes=40 * 1024 * 1024
+        ),
+    )(need_lists, outgoing)
 
 
 def body(
@@ -38,24 +201,7 @@
     width = down_weight.shape[2]
     tokens = residual.shape[0]
     listed = lax.dynamic_index_in_dim(need_lists, column, 0, keepdims=False)
-    owner_of = need_lists // held
-    local_of = need_lists % held
-    mine = owner_of == column
-    has_one = jnp.any(mine, axis=1)
-    local_pick = jnp.sum(jnp.where(mine, local_of, 0), axis=1)
-    owned = jnp.stack(
-        [gate_up_weight[:, :, :width], gate_up_weight[:, :, width:], down_weight], axis=2
-    )
-    outgoing = jnp.where(
-        has_one[:, None, None, None],
-        jnp.take(owned, local_pick, axis=0),
-        jnp.zeros((), jnp.bfloat16),
-    )
-    arrived = lax.all_to_all(outgoing, "expert", split_axis=0, concat_axis=0, tiled=True)
-    slot_rows = jnp.take(arrived, listed // held, axis=0)
-    spread_out = jnp.broadcast_to(slot_rows[None], (ranks // 2,) + slot_rows.shape).reshape(
-        (ranks,) + slot_rows.shape[1:]
-    )
+    outgoing = pick(need_lists, gate_up_weight, down_weight)
     stream_in = residual.astype(jnp.float32)
     factor_in = norm_factor(stream_in)
     normed = (stream_in * factor_in * expert_gain).astype(jnp.bfloat16)
@@ -70,16 +216,16 @@
     send_grad = (mix_there[:, None] * grad_out).astype(jnp.bfloat16)
     partner_normed, partner_grad = partner((normed, send_grad), "dp", 0)
     pair_normed = jnp.concatenate([normed, partner_normed], axis=0)
-    weights = lax.all_to_all(spread_out, "dp", split_axis=0, concat_axis=1, tiled=True)[0]
-    hidden = jnp.einsum(
-        "td,dkf->tkf", pair_normed, weights[:, :2], preferred_element_type=jnp.float32
-    )
-    gate_part = hidden[:, 0]
-    up_part = hidden[:, 1]
+    weights = move(need_lists, outgoing, held, ranks)
+    gate_up = weights[:, : 2 * width]
+    down = weights[:, 2 * width :]
+    hidden = jnp.dot(pair_normed, gate_up, preferred_element_type=jnp.float32)
+    gate_part = hidden[:, :width]
+    up_part = hidden[:, width:]
     sigma = jax.nn.sigmoid(gate_part)
     silu_gate = gate_part * sigma
     act = (silu_gate * up_part).astype(jnp.bfloat16)
-    branch = jnp.einsum("tf,df->td", act, weights[:, 2], preferred_element_type=jnp.float32).astype(
+    branch = jnp.einsum("tf,df->td", act, down, preferred_element_type=jnp.float32).astype(
         jnp.bfloat16
     )
     other_branch = partner(branch[tokens:], "dp", 0)
@@ -98,15 +244,13 @@
     grad_branch = jnp.concatenate(
         [(mix_here[:, None] * grad_out).astype(jnp.bfloat16), partner_grad], axis=0
     )
-    grad_act = jnp.einsum(
-        "td,df->tf", grad_branch, weights[:, 2], preferred_element_type=jnp.float32
-    )
+    grad_act = jnp.einsum("td,df->tf", grad_branch, down, preferred_element_type=jnp.float32)
     slope = sigma * (1.0 + gate_part * (1.0 - sigma))
-    grad_hidden = jnp.stack([grad_act * up_part * slope, grad_act * silu_gate], axis=1).astype(
-        jnp.bfloat16
-    )
+    grad_hidden = jnp.concatenate(
+        [grad_act * up_part * slope, grad_act * silu_gate], axis=1
+    ).astype(jnp.bfloat16)
     expert_term = jnp.einsum(
-        "tkf,dkf->td", grad_hidden, weights[:, :2], preferred_element_type=jnp.float32
+        "tk,dk->td", grad_hidden, gate_up, preferred_element_type=jnp.float32
     ).astype(jnp.bfloat16)
     other_term = partner(expert_term[tokens:], "dp", 0)
     grad_gates = grad_mix * select

time: 290 us -> 315 us (1.086)
  the two profiles are of different devices: /device:TPU:0 before, /device:TPU:27 now
where the time goes in v1:
time: 315 us
  Pallas kernels  280 us (89%)
  matrix products  15.4 us (5%)
  local copies, waits for them, and re-layouts  9.02 us (3%)
  other arithmetic  4.85 us (2%)
  waiting for transfers between devices  3.21 us (1%)
    pallas_call x1, Pallas kernels, pick(): pl.pallas_call(functools.partial(pick_kernel, columns, slots), out_shape=...  145 us
    pallas_call x1, Pallas kernels, move(): pl.pallas_call(functools.partial(move_kernel, columns, ranks, held, chunk...  135 us
    unnamed x29, local copies, waits for them, and re-layouts  7.36 us
  transfers between devices with their start and end apart: 4, of which 3 were waited for; matrix products, arithmetic and copies ran while one was open for 1% of the time, Pallas kernels for 89%

profile of v1, /device:TPU:27, one launch (start us, length us, event | category | flops | bytes accessed | tf_op | source)
XLA Modules:
  0.0 314.6 jit_solution(16198157054040834746)
XLA Ops:
  0.6 0.0 copy-start
  0.6 1.3 fusion.16
  1.9 1.2 fusion.18
  3.2 0.0 copy-start.6
  3.2 0.7 collective-permute-start
  3.9 1.3 copy.11.need_ref
  5.3 0.0 copy-start.3
  5.3 144.9 %shard_map.95.out_ref = bf16[4,256,2304]{2,1,0:T(8,128)(2,1)} custom-call(s32[4,2]{1,0:T(4,128)} %copy.11.need_ref, bf16[8,256,1536]{2,1,0:T(8,128)(2,1)} %gate_up_ref.1, bf16[8,256,768]{2,1,0:T(8,128)(2,1)} %down_ref.1), custom_call_target="tpu_custom_call" | custom-call | tf_op jit(solution)/shard_map/pallas_call | solution.py:60
  150.2 0.0 copy-done.3
  150.2 0.0 copy-start.1
  150.2 2.3 copy-done.1
  152.6 0.0 copy-start.9
  152.6 134.6 %shard_map.96 = bf16[2048,2304]{1,0:T(8,128)(2,1)S(1)} custom-call(s32[4,2]{1,0:T(4,128)S(1)} %copy-done.3, bf16[4,256,2304]{2,1,0:T(8,128)(2,1)S(1)} %copy-done.1), custom_call_target="tpu_custom_call" | custom-call | tf_op jit(solution)/shard_map/pallas_call | solution.py:164
  287.1 0.0 copy-start.2
  287.1 3.6 %copy-done.2 = bf16[2048,2304]{1,0:T(8,128)(2,1)} copy-done((bf16[2048,2304]{1,0:T(8,128)(2,1)}, bf16[2048,2304]{1,0:T(8,128)(2,1)S(1)}, u32[]{:S(2)}) %copy-start.2) | copy-done | bytes 9437208
  290.8 0.0 copy-done.9
  290.8 0.2 dynamic-slice_reduce_fusion
  291.0 0.0 collective-permute-done
  291.0 0.0 copy-done.6
  291.0 4.6 %fusion.2 = f32[256,1536]{1,0:T(8,128)S(1)} fusion(bf16[2048,2304]{1,0:T(8,128)(2,1)} %copy-done.2, bf16[128,2048]{1,0:T(8,128)(2,1)S(1)} %collective-permute-done, bf16[128,2048]{1,0:T(8,128)(2,1)S(1)} %fusion.18), kind=kOutput, calls=%fused_computation.3 | convolution fusion | flops 1612709888 | bytes 8912896 | tf_op jit(solution)/shard_map/dot_general | solution.py:222
  295.6 0.0 copy-start.10
  295.6 3.5 %fusion.11 = bf16[256,2048]{1,0:T(8,128)(2,1)S(1)} fusion(bf16[2048,2304]{1,0:T(8,128)(2,1)} %copy-done.2, f32[256,1536]{1,0:T(8,128)S(1)} %fusion.2), kind=kOutput, calls=%fused_computation.10 | convolution fusion | flops 807010304 | bytes 5767168 | tf_op jit(solution)/shard_map/tf,df->td/dot_general | solution.py:228
  299.1 0.0 copy-start.5
  299.1 0.0 slice-start
  299.1 0.8 slice.37
  300.0 0.0 collective-permute-start.1
  300.0 0.0 copy-done.10
  300.0 0.0 copy-done
  300.0 0.0 copy-start.8
  300.0 0.6 gather_fusion
  300.6 1.3 fusion.50
  301.9 0.0 slice-start.1
  302.0 0.1 collective-permute-done.1
  302.1 0.0 copy-done.5
  302.1 0.3 fusion.25
  302.4 0.0 copy-done.8
  302.5 0.2 fusion.22
  302.7 0.5 collective-permute-start.2
  303.2 1.5 collective-permute-done.2
  304.7 0.0 slice-start.2
  304.7 3.6 %multiply_convert_fusion.1 = (bf16[256,768]{1,0:T(8,128)(2,1)S(1)}, bf16[256,768]{1,0:T(8,128)(2,1)S(1)}) fusion(f32[256,1536]{1,0:T(8,128)} %copy-done.10, bf16[2048,2304]{1,0:T(8,128)(2,1)} %copy-done.2, bf16[128,2048]{1,0:T(8,128)(2,1)S(1)} %collective-permute-done.2, bf16[128,2048]{1,0:T(8,128)(2,1)S(1)} %get-tuple-element.10), kind=kOutput, calls=%fused_computation.47 | convolution fusion | flops 809959424 | bytes 6553600 | tf_op jit(solution)/shard_map/td,df->tf/dot_general | solution.py:247
  308.3 0.0 slice-done
  308.3 0.0 slice-done.1
  308.3 0.0 slice-done.2
  308.4 0.0 copy-start.4
  308.4 0.0 copy-start.7
  308.4 1.9 fusion.8
  310.3 0.4 collective-permute-start.3
  310.8 1.5 collective-permute-done.3
  312.3 0.0 copy-done.4
  312.3 0.0 copy-done.7
  312.3 0.5 fusion.21
  312.9 1.7 fusion.26
  (11 shorter events, 0.1 us)
Async XLA Ops:
  0.6 299.4 %copy-start = (bf16[2048,32]{0,1:T(8,128)(2,1)S(1)}, bf16[2048,32]{0,1:T(8,128)(2,1)}, u32[]{:S(2)}) copy-start(bf16[2048,32]{0,1:T(8,128)(2,1)} %param.11) | copy-start | bytes 393220
  3.2 287.8 %copy-start.6 = (bf16[128,2048]{1,0:T(8,128)(2,1)}, bf16[128,2048]{1,0:T(8,128)(2,1)S(1)}, u32[]{:S(2)}) copy-start(bf16[128,2048]{1,0:T(8,128)(2,1)S(1)} %fusion.18) | copy-start | bytes 1572868
  3.2 287.8 %collective-permute-start = (bf16[128,2048]{1,0:T(8,128)(2,1)S(1)}, bf16[128,2048]{1,0:T(8,128)(2,1)S(1)}, u32[]{:S(2)}, u32[]{:S(2)}) collective-permute-start(bf16[128,2048]{1,0:T(8,128)(2,1)S(1)} %fusion.18), channel_id=1, source_target_pairs={{0,4},{4,0},{8,12},{12,8},{16,20},{20,16},{24,28},{28,24},{1,5},{5... | collective-permute-start | bytes 1572872 | tf_op jit(solution)/shard_map/ppermute | solution.py:17
  5.3 145.0 %copy-start.3 = (s32[4,2]{1,0:T(4,128)S(1)}, s32[4,2]{1,0:T(4,128)}, u32[]{:S(2)}) copy-start(s32[4,2]{1,0:T(4,128)} %copy.11.need_ref) | copy-start | bytes 100
  150.2 2.3 copy-start.1
  152.6 138.2 %copy-start.9 = (s32[4,2]{0,1:T(2,128)S(1)}, s32[4,2]{0,1:T(2,128)}, u32[]{:S(2)}) copy-start(s32[4,2]{0,1:T(2,128)} %param.14) | copy-start | bytes 100
  287.1 3.6 %copy-start.2 = (bf16[2048,2304]{1,0:T(8,128)(2,1)}, bf16[2048,2304]{1,0:T(8,128)(2,1)S(1)}, u32[]{:S(2)}) copy-start(bf16[2048,2304]{1,0:T(8,128)(2,1)S(1)} %shard_map.96) | copy-start | bytes 28311556
  295.6 4.4 %copy-start.10 = (f32[256,1536]{1,0:T(8,128)}, f32[256,1536]{1,0:T(8,128)S(1)}, u32[]{:S(2)}) copy-start(f32[256,1536]{1,0:T(8,128)S(1)} %fusion.2) | copy-start | bytes 4718596
  299.1 3.0 copy-start.5
  299.1 9.2 %slice-start = ((s8[9437184]{0:T(1024)(128)(4,1)}), s8[1048576]{0:T(1024)(128)(4,1)S(1)}, s32[]{:S(2)}) async-start(s8[9437184]{0:T(1024)(128)(4,1)} %bitcast.12), calls=%async_computation | async-start | bytes 2097152
  300.0 2.1 collective-permute-start.1
  300.0 2.4 copy-start.8
  301.9 6.4 %slice-start.1 = ((s8[9437184]{0:T(1024)(128)(4,1)}), s8[4194304]{0:T(1024)(128)(4,1)S(1)}, s32[]{:S(2)}) async-start(s8[9437184]{0:T(1024)(128)(4,1)} %bitcast.12), calls=%async_computation.1 | async-start | bytes 8388608
  302.7 2.0 collective-permute-start.2
  304.7 3.6 %slice-start.2 = ((s8[9437184]{0:T(1024)(128)(4,1)}), s8[4194304]{0:T(1024)(128)(4,1)S(1)}, s32[]{:S(2)}) async-start(s8[9437184]{0:T(1024)(128)(4,1)} %bitcast.12), calls=%async_computation.2 | async-start | bytes 8388608
  308.4 3.9 %copy-start.4 = (bf16[128,2048]{1,0:T(8,128)(2,1)S(1)}, bf16[128,2048]{1,0:T(8,128)(2,1)}, u32[]{:S(2)}) copy-start(bf16[128,2048]{1,0:T(8,128)(2,1)} %param.8) | copy-start | bytes 1572868
  308.4 3.9 %copy-start.7 = (f32[2048]{0:T(1024)S(1)}, f32[2048]{0:T(1024)}, u32[]{:S(2)}) copy-start(f32[2048]{0:T(1024)} %param.10) | copy-start | bytes 24580
  310.3 2.0 collective-permute-start.3

commit v2 on v0

v2 whole, which is shorter than its diff:
```python
import functools

import jax
import jax.numpy as jnp
from jax import lax
from jax.experimental import pallas as pl
from jax.experimental.pallas import tpu as pltpu
from jax.sharding import PartitionSpec as P

eps = 1e-05
MESH = pl.DeviceIdType.MESH


def norm_factor(values):
    return lax.rsqrt(jnp.mean(values * values, axis=-1, keepdims=True) + eps)


def norm_backward(values, factor, gain, grad):
    scaled = gain * grad
    return factor * scaled - values * factor**3 * jnp.mean(values * scaled, axis=-1, keepdims=True)


def block_kernel(
    columns,
    ranks,
    need_ref,
    gate_up_ref,
    down_ref,
    normed_ref,
    grad_here_ref,
    grad_there_ref,
    branch_here,
    branch_there,
    term_here,
    term_there,
    *scratch,
):
    held, rows, _ = down_ref.shape
    width = down_ref.shape[2]
    slice_ = 128
    parts = width // slice_
    tokens = normed_ref.shape[0]
    local = scratch[:parts]
    arrived = scratch[parts : 2 * parts]
    (src, stage, weights, pair_x, pair_g, sum_b, sum_t, back_b, back_t) = scratch[
        2 * parts : 2 * parts + 9
    ]
    ld, zs, zr, ps, pr, ts, tr = scratch[2 * parts + 9 :]
    column = lax.axis_index("expert")
    me = lax.axis_index("dp")
    core = lax.rem(me, 2)
    sibling = me + 1 - 2 * core
    square = ranks == 8
    depth = 2

    def loads(c):
        return [
            pltpu.make_async_copy(
                ref.at[:, :, pl.ds(start, slice_)],
                local[c].at[:, :, pl.ds(i * slice_, slice_)],
                ld.at[c, i],
            )
            for i, (ref, start) in enumerate(
                (
                    (gate_up_ref, c * slice_),
                    (gate_up_ref, width + c * slice_),
                    (down_ref, c * slice_),
                )
            )
        ]

    for c in range(parts):
        for copy in loads(c):
            copy.start()

    if square:
        beside = me + 2 - 4 * lax.rem(me // 2, 2)
        across = me + 4 - 8 * (me // 4)
        peers = [sibling, beside, across]
    else:
        peers = [lax.rem(me + k, ranks) for k in range(1, ranks)]
    barrier = pltpu.get_barrier_semaphore()
    for k in range(1, columns):
        pl.semaphore_signal(
            barrier, inc=1, device_id=(me, lax.rem(column + k, columns)), device_id_type=MESH
        )
    for peer in peers:
        pl.semaphore_signal(barrier, inc=1, device_id=(peer, column), device_id_type=MESH)
    pl.semaphore_wait(barrier, columns - 1 + len(peers))

    def to_sibling(i, source, target):
        return pltpu.make_async_remote_copy(
            src_ref=source,
            dst_ref=target,
            send_sem=ts.at[i],
            recv_sem=tr.at[i],
            device_id=(sibling, column),
            device_id_type=MESH,
        )

    def token_copies():
        return [
            to_sibling(0, normed_ref, pair_x.at[pl.ds(tokens, tokens)]),
            to_sibling(1, grad_there_ref, pair_g.at[pl.ds(tokens, tokens)]),
        ]

    for copy in token_copies():
        copy.start()

    def column_copy(c, k):
        return pltpu.make_async_remote_copy(
            src_ref=src.at[c, k - 1],
            dst_ref=arrived[c].at[column],
            send_sem=zs.at[k - 1, c],
            recv_sem=zr.at[k - 1, c],
            device_id=(me, lax.rem(column + k, columns)),
            device_id_type=MESH,
        )

    def pick(to):
        found = jnp.int32(0)
        for s in range(2):
            expert = need_ref[to, s]
            found = jnp.where(expert // held == column, expert % held, found)
        return found

    picks = [pick(lax.rem(column + k, columns)) for k in range(columns)]
    owner_mine = need_ref[column, core] // held
    owner_other = need_ref[column, 1 - core] // held

    def start_columns(c):
        for copy in loads(c):
            copy.wait()
        for k in range(1, columns):
            src[c, k - 1] = local[c][picks[k]]
            column_copy(c, k).start()
        arrived[c][column] = local[c][picks[0]]

    def block(c, rank):
        return weights.at[c, pl.ds(pl.multiple_of(rank * rows, rows), rows)]

    def spread(c, i, source, rank, to):
        return pltpu.make_async_remote_copy(
            src_ref=source,
            dst_ref=block(c, rank),
            send_sem=ps.at[i, c],
            recv_sem=pr.at[i, c],
            device_id=(to, column),
            device_id_type=MESH,
        )

    if square:
        beside_rank = beside
        across_other = across + 1 - 2 * core

        def spreads(c):
            mine, other = block(c, me), stage.at[c]
            return [
                spread(c, 0, other, me, sibling),
                spread(c, 1, mine, me, beside),
                spread(c, 2, mine, me, across),
                spread(c, 3, block(c, sibling), sibling, beside),
                spread(c, 4, block(c, sibling), sibling, across),
                spread(c, 5, block(c, beside_rank), beside_rank, across),
                spread(c, 6, block(c, across_other), across_other, beside),
            ]

        def first(c):
            copies = spreads(c)
            for i in (0, 1, 2):
                copies[i].start()

        def second(c):
            copies = spreads(c)
            copies[0].wait_recv()
            copies[3].start()
            copies[4].start()

        def third(c):
            copies = spreads(c)
            copies[1].wait_recv()
            copies[5].start()
            copies[4].wait_recv()
            copies[6].start()

        def last(c):
            copies = spreads(c)
            for i in (2, 3, 5, 6):
                copies[i].wait_recv()
    else:

        def spreads(c):
            return [
                spread(
                    c,
                    k - 1,
                    block(c, me) if k % 2 == 0 else stage.at[c],
                    me,
                    lax.rem(me + k, ranks),
                )
                for k in range(1, ranks)
            ]

        def first(c):
            for copy in spreads(c):
                copy.start()

        def second(c):
            pass

        def third(c):
            pass

        def last(c):
            for copy in spreads(c):
                copy.wait_recv()

    def dot(left, right):
        return jnp.dot(left, right, preferred_element_type=jnp.float32)

    def dot_t(left, right):
        return lax.dot_general(
            left, right, (((1,), (1,)), ((), ())), preferred_element_type=jnp.float32
        )

    def work(c):
        hidden = dot(pair_x[...], weights[c, :, : 2 * slice_])
        grad_act = dot(pair_g[...], weights[c, :, 2 * slice_ :])
        gate_part = hidden[:, :slice_]
        up_part = hidden[:, slice_:]
        sigma = jax.nn.sigmoid(gate_part)
        silu_gate = gate_part * sigma
        act = (silu_gate * up_part).astype(jnp.bfloat16)
        slope = sigma * (1.0 + gate_part * (1.0 - sigma))
        grad_hidden = jnp.concatenate(
            [grad_act * up_part * slope, grad_act * silu_gate], axis=1
        ).astype(jnp.bfloat16)
        branch = dot_t(act, weights[c, :, 2 * slice_ :])
        term = dot_t(grad_hidden, weights[c, :, : 2 * slice_])
        if c == 0:
            sum_b[...] = branch
            sum_t[...] = term
        else:
            sum_b[...] += branch
            sum_t[...] += term

    for c in range(min(depth, parts)):
        start_columns(c)
    pair_x[pl.ds(0, tokens)] = normed_ref[...]
    pair_g[pl.ds(0, tokens)] = grad_here_ref[...]
    for c in range(parts + 2):
        if c < parts:
            for k in range(1, columns):
                column_copy(c, k).wait_recv()
            weights[c, pl.ds(pl.multiple_of(me * rows, rows), rows)] = arrived[c][owner_mine]
            stage[c] = arrived[c][owner_other]
            first(c)
            if c + depth < parts:
                start_columns(c + depth)
            second(c)
        if 1 <= c <= parts:
            third(c - 1)
        if c >= 2:
            last(c - 2)
            if c == 2:
                for copy in token_copies():
                    copy.wait()
            work(c - 2)

    back_b[...] = sum_b[pl.ds(tokens, tokens)].astype(jnp.bfloat16)
    back_t[...] = sum_t[pl.ds(tokens, tokens)].astype(jnp.bfloat16)
    backs = [to_sibling(2, back_b, branch_there), to_sibling(3, back_t, term_there)]
    for copy in backs:
        copy.start()
    branch_here[...] = sum_b[pl.ds(0, tokens)].astype(jnp.bfloat16)
    term_here[...] = sum_t[pl.ds(0, tokens)].astype(jnp.bfloat16)
    for c in range(parts):
        for k in range(1, columns):
            column_copy(c, k).wait_send()
        for copy in spreads(c):
            copy.wait_send()
    for copy in backs:
        copy.wait()


def experts(need_lists, gate_up_weight, down_weight, normed, grad_here, grad_there, ranks):
    columns = need_lists.shape[0]
    held, rows, width = down_weight.shape
    tokens, model = normed.shape
    slice_ = 128
    parts = width // slice_
    vmem = pl.BlockSpec(memory_space=pltpu.VMEM)
    any_ = pl.BlockSpec(memory_space=pl.ANY)
    sent = 7 if ranks == 8 else ranks - 1
    bf16, f32 = jnp.bfloat16, jnp.float32
    return pl.pallas_call(
        functools.partial(block_kernel, columns, ranks),
        out_shape=[jax.ShapeDtypeStruct((tokens, model), bf16)] * 4,
        in_specs=[pl.BlockSpec(memory_space=pltpu.SMEM), any_, any_, vmem, vmem, vmem],
        out_specs=[vmem] * 4,
        scratch_shapes=[pltpu.VMEM((held, rows, 3 * slice_), bf16) for _ in range(parts)]
        + [pltpu.VMEM((columns, rows, 3 * slice_), bf16) for _ in range(parts)]
        + [
            pltpu.VMEM((parts, columns - 1, rows, 3 * slice_), bf16),
            pltpu.VMEM((parts, rows, 3 * slice_), bf16),
            pltpu.VMEM((parts, ranks * rows, 3 * slice_), bf16),
            pltpu.VMEM((2 * tokens, model), bf16),
            pltpu.VMEM((2 * tokens, model), bf16),
            pltpu.VMEM((2 * tokens, model), f32),
            pltpu.VMEM((2 * tokens, model), f32),
            pltpu.VMEM((tokens, model), bf16),
            pltpu.VMEM((tokens, model), bf16),
            pltpu.SemaphoreType.DMA((parts, 3)),
            pltpu.SemaphoreType.DMA((columns - 1, parts)),
            pltpu.SemaphoreType.DMA((columns - 1, parts)),
            pltpu.SemaphoreType.DMA((sent, parts)),
            pltpu.SemaphoreType.DMA((sent, parts)),
            pltpu.SemaphoreType.DMA((4,)),
            pltpu.SemaphoreType.DMA((4,)),
        ],
        compiler_params=pltpu.CompilerParams(
            collective_id=0, has_side_effects=True, vmem_limit_bytes=56 * 1024 * 1024
        ),
    )(need_lists, gate_up_weight, down_weight, normed, grad_here, grad_there)


def body(
    residual,
    grad_stream,
    expert_gain,
    router_weight,
    gate_up_weight,
    down_weight,
    need_lists,
    routes,
):
    column = lax.axis_index("expert")
    ranks = lax.axis_size("dp")
    parity = lax.axis_index("dp") % 2
    listed = lax.dynamic_index_in_dim(need_lists, column, 0, keepdims=False)
    stream_in = residual.astype(jnp.float32)
    factor_in = norm_factor(stream_in)
    normed = (stream_in * factor_in * expert_gain).astype(jnp.bfloat16)
    router_cols = jnp.take(router_weight, listed, axis=1)
    logits = jnp.dot(normed, router_cols, preferred_element_type=jnp.float32)
    gates = jax.nn.sigmoid(logits - logits[:, ::-1])
    select = (routes == jnp.arange(2, dtype=jnp.int32)[None, :]).astype(jnp.float32)
    mix = gates * select
    mix_here = lax.dynamic_index_in_dim(mix, parity, 1, keepdims=False)
    mix_there = lax.dynamic_index_in_dim(mix, 1 - parity, 1, keepdims=False)
    grad_out = grad_stream.astype(jnp.float32)
    grad_here = (mix_here[:, None] * grad_out).astype(jnp.bfloat16)
    grad_there = (mix_there[:, None] * grad_out).astype(jnp.bfloat16)
    branch_here, branch_there, term_here, term_there = experts(
        need_lists, gate_up_weight, down_weight, normed, grad_here, grad_there, ranks
    )
    branch_here = branch_here.astype(jnp.float32)
    branch_there = branch_there.astype(jnp.float32)
    stream = (
        stream_in + mix_here[:, None] * branch_here + mix_there[:, None] * branch_there
    ).astype(jnp.bfloat16)
    mix_grad_here = jnp.sum(branch_here * grad_out, axis=-1)
    mix_grad_there = jnp.sum(branch_there * grad_out, axis=-1)
    grad_mix = jnp.where(
        parity == 0,
        jnp.stack([mix_grad_here, mix_grad_there], axis=1),
        jnp.stack([mix_grad_there, mix_grad_here], axis=1),
    )
    grad_gates = grad_mix * select
    grad_logits = (
        gates * (grad_gates - jnp.sum(gates * grad_gates, axis=-1, keepdims=True))
    ).astype(jnp.bfloat16)
    grad_normed = term_here.astype(jnp.float32) + term_there.astype(jnp.float32)
    grad_normed = grad_normed + jnp.einsum(
        "tn,dn->td", grad_logits, router_cols, preferred_element_type=jnp.float32
    )
    grad_residual = (
        grad_out + norm_backward(stream_in, factor_in, expert_gain, grad_normed)
    ).astype(jnp.bfloat16)
    return (stream, grad_residual)


def solution(mesh):
    return jax.shard_map(
        body,
        mesh=mesh,
        in_specs=(
            P(("dp", "expert"), None),
            P(("dp", "expert"), None),
            P(),
            P(),
            P("expert", "dp", None),
            P("expert", "dp", None),
            P(),
            P(("dp", "expert"), None),
        ),
        out_specs=(P(("dp", "expert"), None), P(("dp", "expert"), None)),
        check_vma=False,
    )
```

time: 290 us -> 154 us (0.53)
  the two profiles are of different devices: /device:TPU:0 before, /device:TPU:25 now
where the time goes in v2:
time: 154 us
  Pallas kernels  140 us (91%)
  other arithmetic  7.79 us (5%)
  local copies, waits for them, and re-layouts  2.92 us (2%)
  matrix products  2 us (1%)
    pallas_call x1, Pallas kernels, experts(): pl.pallas_call(functools.partial(block_kernel, columns, ranks), out_shape...  140 us

profile of v2, /device:TPU:25, one launch (start us, length us, event | category | flops | bytes accessed | tf_op | source)
XLA Modules:
  0.0 153.8 jit_solution(13759534447685401472)
XLA Ops:
  0.6 0.0 copy-start
  0.6 0.0 copy-start.2
  0.7 0.0 copy-start.5
  0.7 0.9 dynamic-slice_reduce_fusion
  1.6 1.2 fusion.3
  2.9 1.3 copy.10.need_ref
  4.2 0.0 copy-done
  4.2 0.6 gather_fusion
  4.8 1.2 fusion.5.normed_ref
  6.0 0.0 copy-start.3
  6.1 0.3 fusion.21
  6.4 0.0 copy-done.5
  6.4 0.0 copy-done.2
  6.4 0.0 copy-start.1
  6.4 1.2 fusion.10
  7.6 0.0 copy-done.3
  7.6 0.0 copy-start.4
  7.6 140.3 %shard_map.95 = (bf16[128,2048]{1,0:T(8,128)(2,1)}, bf16[128,2048]{1,0:T(8,128)(2,1)}, bf16[128,2048]{1,0:T(8,128)(2,1)}, bf16[128,2048]{1,0:T(8,128)(2,1)}) custom-call(s32[4,2]{1,0:T(4,128)} %copy.10.need_ref, bf16[8,256,1536]{2,1,0:T(8,128)(2,1)} %gate_up_ref.1, bf16[8,256,768]{2,1,0:T(8,128)(2,1)} %down_ref.1, bf16[128,2048]{1,0:T(8,128)(2,1)} %copy-done.3, ...), custom_call_target="tpu_custom_call" | custom-call | tf_op jit(solution)/shard_map/pallas_call | solution.py:296
  148.0 0.0 copy-done.1
  148.0 2.8 %fusion.12 = (f32[128]{0:T(128)S(1)}, f32[128]{0:T(128)S(1)}, bf16[128,2048]{1,0:T(8,128)(2,1)}) fusion(bf16[128,2048]{1,0:T(8,128)(2,1)S(1)} %copy-done.2, bf16[128,2048]{1,0:T(8,128)(2,1)} %get-tuple-element.7, bf16[128,2048]{1,0:T(8,128)(2,1)} %get-tuple-element.6, f32[128]{0:T(128)S(1)} %get-tuple-element.17, f32[128]{0:T(128)S(1)} %get-tuple-element.18, ...), kind=kLoop, calls=%fused_computation.26 | loop fusion | flops 3407616 | bytes 2623488 | tf_op jit(solution)/shard_map/reduce_sum | solution.py:363
  150.8 0.0 copy-done.4
  150.8 1.7 %fusion.8 = (f32[128]{0:T(128)S(1)}, f32[128,2048]{1,0:T(8,128)S(1)}) fusion(bf16[128,2048]{1,0:T(8,128)(2,1)S(1)} %copy-done.1, bf16[2,2048]{1,0:T(2,128)(2,1)S(1)} %gather_fusion, pred[2]{0:T(512)(128)(4,1)S(1)} %compare_and_fusion, f32[128,2]{0,1:T(2,128)S(1)} %get-tuple-element.13, f32[128]{0:T(128)S(1)} %multiply_reduce_fusion, ...), kind=kOutput, calls=%fused_computation.22 | convolution fusion | flops 3151744 | bytes 2641411 | tf_op jit(solution)/shard_map/tn,dn->td/dot_general | solution.py:374
  152.5 1.3 fusion.13
  (9 shorter events, 0.1 us)
Async XLA Ops:
  0.6 3.6 %copy-start = (bf16[2048,32]{0,1:T(8,128)(2,1)S(1)}, bf16[2048,32]{0,1:T(8,128)(2,1)}, u32[]{:S(2)}) copy-start(bf16[2048,32]{0,1:T(8,128)(2,1)} %param.11) | copy-start | bytes 393220
  0.6 5.8 %copy-start.2 = (bf16[128,2048]{1,0:T(8,128)(2,1)S(1)}, bf16[128,2048]{1,0:T(8,128)(2,1)}, u32[]{:S(2)}) copy-start(bf16[128,2048]{1,0:T(8,128)(2,1)} %param.9) | copy-start | bytes 1572868
  0.7 5.7 %copy-start.5 = (s32[128,1]{0,1:T(1,128)S(1)}, s32[128,1]{0,1:T(1,128)}, u32[]{:S(2)}) copy-start(s32[128,1]{0,1:T(1,128)} %param.15) | copy-start | bytes 1540
  6.0 1.6 %copy-start.3 = (bf16[128,2048]{1,0:T(8,128)(2,1)}, bf16[128,2048]{1,0:T(8,128)(2,1)S(1)}, u32[]{:S(2)}) copy-start(bf16[128,2048]{1,0:T(8,128)(2,1)S(1)} %fusion.5.normed_ref) | copy-start | bytes 1572868
  6.4 141.5 %copy-start.1 = (bf16[128,2048]{1,0:T(8,128)(2,1)S(1)}, bf16[128,2048]{1,0:T(8,128)(2,1)}, u32[]{:S(2)}) copy-start(bf16[128,2048]{1,0:T(8,128)(2,1)} %param.8) | copy-start | bytes 1572868
  7.6 143.1 %copy-start.4 = (f32[2048]{0:T(1024)S(1)}, f32[2048]{0:T(1024)}, u32[]{:S(2)}) copy-start(f32[2048]{0:T(1024)} %param.10) | copy-start | bytes 24580

commit v3 on v2

--- a/solution.py
+++ b/solution.py
@@ -23,6 +23,7 @@
 def block_kernel(
     columns,
     ranks,
+    relays,
     need_ref,
     gate_up_ref,
     down_ref,
@@ -117,14 +118,46 @@
             device_id_type=MESH,
         )
 
-    def pick(to):
-        found = jnp.int32(0)
+    def pick(to, found):
         for s in range(2):
             expert = need_ref[to, s]
             found = jnp.where(expert // held == column, expert % held, found)
         return found
 
-    picks = [pick(lax.rem(column + k, columns)) for k in range(columns)]
+    picks = []
+    for k in range(columns):
+        to = lax.rem(column + k, columns)
+        found = jnp.int32(0)
+        for owner, via, end in relays:
+            if (via - owner) % columns == k:
+                found = jnp.where(column == owner, pick(end, found), found)
+        picks.append(pick(to, found))
+
+    def sends(k):
+        yes = column >= 0
+        for owner, via, end in relays:
+            if (end - owner) % columns == k:
+                yes = yes & (column != owner)
+        return yes
+
+    def relay_copy(c, i):
+        owner, via, end = relays[i]
+        return pltpu.make_async_remote_copy(
+            src_ref=arrived[c].at[owner],
+            dst_ref=arrived[c].at[owner],
+            send_sem=zs.at[columns - 1, c],
+            recv_sem=zr.at[(end - owner) % columns - 1, c],
+            device_id=(me, end),
+            device_id_type=MESH,
+        )
+
+    def relay(c, act):
+        for i, (owner, via, end) in enumerate(relays):
+
+            @pl.when(column == via)
+            def _():
+                act(relay_copy(c, i))
+
     owner_mine = need_ref[column, core] // held
     owner_other = need_ref[column, 1 - core] // held
 
@@ -133,7 +166,11 @@
             copy.wait()
         for k in range(1, columns):
             src[c, k - 1] = local[c][picks[k]]
-            column_copy(c, k).start()
+
+            @pl.when(sends(k))
+            def _():
+                column_copy(c, k).start()
+
         arrived[c][column] = local[c][picks[0]]
 
     def block(c, rank):
@@ -252,6 +289,7 @@
         if c < parts:
             for k in range(1, columns):
                 column_copy(c, k).wait_recv()
+            relay(c, lambda copy: copy.start())
             weights[c, pl.ds(pl.multiple_of(me * rows, rows), rows)] = arrived[c][owner_mine]
             stage[c] = arrived[c][owner_other]
             first(c)
@@ -276,14 +314,19 @@
     term_here[...] = sum_t[pl.ds(0, tokens)].astype(jnp.bfloat16)
     for c in range(parts):
         for k in range(1, columns):
-            column_copy(c, k).wait_send()
+
+            @pl.when(sends(k))
+            def _():
+                column_copy(c, k).wait_send()
+
+        relay(c, lambda copy: copy.wait_send())
         for copy in spreads(c):
             copy.wait_send()
     for copy in backs:
         copy.wait()
 
 
-def experts(need_lists, gate_up_weight, down_weight, normed, grad_here, grad_there, ranks):
+def experts(ranks, relays, number, need_lists, gate_up_weight, down_weight, normed, grad_here, grad_there):
     columns = need_lists.shape[0]
     held, rows, width = down_weight.shape
     tokens, model = normed.shape
@@ -294,7 +337,7 @@
     sent = 7 if ranks == 8 else ranks - 1
     bf16, f32 = jnp.bfloat16, jnp.float32
     return pl.pallas_call(
-        functools.partial(block_kernel, columns, ranks),
+        functools.partial(block_kernel, columns, ranks, relays),
         out_shape=[jax.ShapeDtypeStruct((tokens, model), bf16)] * 4,
         in_specs=[pl.BlockSpec(memory_space=pltpu.SMEM), any_, any_, vmem, vmem, vmem],
         out_specs=[vmem] * 4,
@@ -311,7 +354,7 @@
             pltpu.VMEM((tokens, model), bf16),
             pltpu.VMEM((tokens, model), bf16),
             pltpu.SemaphoreType.DMA((parts, 3)),
-            pltpu.SemaphoreType.DMA((columns - 1, parts)),
+            pltpu.SemaphoreType.DMA((columns, parts)),
             pltpu.SemaphoreType.DMA((columns - 1, parts)),
             pltpu.SemaphoreType.DMA((sent, parts)),
             pltpu.SemaphoreType.DMA((sent, parts)),
@@ -319,9 +362,19 @@
             pltpu.SemaphoreType.DMA((4,)),
         ],
         compiler_params=pltpu.CompilerParams(
-            collective_id=0, has_side_effects=True, vmem_limit_bytes=56 * 1024 * 1024
+            collective_id=number, has_side_effects=True, vmem_limit_bytes=56 * 1024 * 1024
         ),
     )(need_lists, gate_up_weight, down_weight, normed, grad_here, grad_there)
+
+
+def fits(need_lists, held, relays):
+    owner_of = need_lists // held
+    good = jnp.bool_(True)
+    for owner, via, end in relays:
+        near = jnp.max(jnp.where(owner_of[via] == owner, need_lists[via], -1))
+        far = jnp.max(jnp.where(owner_of[end] == owner, need_lists[end], -1))
+        good = good & ((near < 0) | (far < 0) | (near == far))
+    return good
 
 
 def body(
@@ -351,8 +404,23 @@
     grad_out = grad_stream.astype(jnp.float32)
     grad_here = (mix_here[:, None] * grad_out).astype(jnp.bfloat16)
     grad_there = (mix_there[:, None] * grad_out).astype(jnp.bfloat16)
-    branch_here, branch_there, term_here, term_there = experts(
-        need_lists, gate_up_weight, down_weight, normed, grad_here, grad_there, ranks
+    plans = [()]
+    if need_lists.shape[0] == 4:
+        plans = [((1, 2, 3), (2, 1, 0)), ((0, 2, 3), (2, 1, 0)), ()]
+    held = gate_up_weight.shape[0]
+    good = [fits(need_lists, held, plan) for plan in plans]
+    choice = jnp.int32(len(plans) - 1)
+    for i in reversed(range(len(plans) - 1)):
+        choice = jnp.where(good[i], i, choice)
+    branch_here, branch_there, term_here, term_there = lax.switch(
+        choice,
+        [functools.partial(experts, ranks, plan, i) for i, plan in enumerate(plans)],
+        need_lists,
+        gate_up_weight,
+        down_weight,
+        normed,
+        grad_here,
+        grad_there,
     )
     branch_here = branch_here.astype(jnp.float32)
     branch_there = branch_there.astype(jnp.float32)

time: 154 us -> 142 us (0.922)
  the two profiles are of different devices: /device:TPU:25 before, /device:TPU:0 now
where the time goes in v3:
time: 142 us
  Pallas kernels  116 us (82%)
  other arithmetic  12.6 us (9%)
  between operations  8.42 us (6%)
  local copies, waits for them, and re-layouts  2.1 us (1%)
  matrix products  1.84 us (1%)
    pallas_call x1, Pallas kernels, experts(): pl.pallas_call(functools.partial(block_kernel, columns, ranks, relays), o...  116 us

profile of v3, /device:TPU:0, one launch (start us, length us, event | category | flops | bytes accessed | tf_op | source)
XLA Modules:
  0.0 141.7 jit_solution(14064715596607835232)
XLA Ops:
  0.6 0.0 copy-start
  0.6 0.0 copy-start.3
  0.7 0.0 copy-start.5
  0.7 0.0 copy-start.1
  0.7 1.4 fusion.3
  2.1 0.7 and_select_fusion
  2.8 1.7 %fusion.19 = (s32[]{:T(128)}, s32[]{:T(128)}, s32[]{:T(128)}, s32[]{:T(128)}, s32[]{:T(128)}, /*index=5*/s32[]{:T(128)}, s32[2]{0:T(128)S(1)}) fusion(s32[4,2]{0,1:T(2,128)} %param.17, s32[4,2]{0,1:T(2,128)S(1)} %and_select_fusion, s32[]{:T(128)S(6)} %select_n.86), kind=kLoop, calls=%fused_computation.48 | loop fusion | flops 30 | bytes 108 | tf_op jit(solution)/shard_map/reduce_max | solution.py:375
  12.2 0.0 copy-done
  12.2 0.6 gather_fusion
  12.8 1.2 fusion.5
  14.0 0.0 copy-start.2
  14.0 0.8 copy-done.2
  14.8 0.3 fusion.27
  15.1 0.0 copy-done.5
  15.2 2.2 %fusion.10 = (bf16[128,2048]{1,0:T(8,128)(2,1)}, bf16[128,2048]{1,0:T(8,128)(2,1)}) fusion(bf16[128,2048]{1,0:T(8,128)(2,1)} %param.12, f32[128]{0:T(128)S(1)} %get-tuple-element.210, f32[128]{0:T(128)S(1)} %get-tuple-element.211), kind=kLoop, calls=%fused_computation.24 | loop fusion | flops 1310720 | bytes 1573888 | tf_op jit(solution)/shard_map/convert_element_type | solution.py:406
  17.4 0.0 copy-done.3
  17.4 0.0 copy-done.1
  17.4 0.0 copy-start.4
  17.4 117.4 %conditional.1 = ((bf16[128,2048]{1,0:T(8,128)(2,1)S(1)}, bf16[128,2048]{1,0:T(8,128)(2,1)S(1)}, bf16[128,2048]{1,0:T(8,128)(2,1)S(1)}, bf16[128,2048]{1,0:T(8,128)(2,1)S(1)})) conditional(s32[]{:T(128)} %clamp.3, (s32[4,2]{0,1:T(2,128)S(1)}, bf16[8,256,1536]{2,1,0:T(8,128)(2,1)}, bf16[8,256,768]{2,1,0:T(8,128)(2,1)S(1)}, ...), branch_computations={%region_7.8_spmd.clone, %region_8.9_spmd.clone, %region_9.10_spmd.... | conditional | bytes 72 | solution.py:415
  17.4 0.7 copy.22.need_ref
  18.1 116.4 %branch_0_fun.2 = (bf16[128,2048]{1,0:T(8,128)(2,1)S(1)}, bf16[128,2048]{1,0:T(8,128)(2,1)S(1)}, bf16[128,2048]{1,0:T(8,128)(2,1)S(1)}, bf16[128,2048]{1,0:T(8,128)(2,1)S(1)}) custom-call(s32[4,2]{1,0:T(4,128)} %copy.22.need_ref, bf16[8,256,1536]{2,1,0:T(8,128)(2,1)} %get-tuple-element.142.gate_up_ref, bf16[8,256,768]{2,1,0:T(8,128)(2,1)S(1)} %get-tuple-element.143.down_ref, ...), custom_call_target="tpu_custom_call" | custom-call | tf_op jit(solution)/shard_map/cond/branch_0_fun/pallas_call | solution.py:339
  134.8 2.8 %fusion.12 = (f32[128]{0:T(128)S(1)}, f32[128]{0:T(128)S(1)}, bf16[128,2048]{1,0:T(8,128)(2,1)}) fusion(bf16[128,2048]{1,0:T(8,128)(2,1)} %param.12, bf16[128,2048]{1,0:T(8,128)(2,1)S(1)} %get-tuple-element.194, bf16[128,2048]{1,0:T(8,128)(2,1)S(1)} %get-tuple-element.195, f32[128]{0:T(128)S(1)} %get-tuple-element.210, f32[128]{0:T(128)S(1)} %get-tuple-element.211, ...), kind=kLoop, calls=%fused_computation.26 | loop fusion | flops 3407616 | bytes 2623488 | tf_op jit(solution)/shard_map/reduce_sum | solution.py:431
  137.6 0.0 copy-done.4
  137.6 1.6 %fusion.8 = (f32[128]{0:T(128)S(1)}, f32[128,2048]{1,0:T(8,128)S(1)}) fusion(bf16[128,2048]{1,0:T(8,128)(2,1)} %param.11, bf16[2,2048]{1,0:T(2,128)(2,1)S(1)} %gather_fusion, pred[2]{0:T(512)(128)(4,1)S(1)} %compare_and_fusion, f32[128,2]{0,1:T(2,128)S(1)} %get-tuple-element.206, f32[128]{0:T(128)S(1)} %multiply_reduce_fusion, f32[128,1]{0,1:T(1,128)S(1)} %bitcast.15, ...), kind=kOutput, calls=%fused_computation.22 | convolution fusion | flops 3151744 | bytes 2641411 | tf_op jit(solution)/shard_map/tn,dn->td/dot_general | solution.py:442
  139.2 2.5 %fusion.13 = bf16[128,2048]{1,0:T(8,128)(2,1)} fusion(bf16[128,2048]{1,0:T(8,128)(2,1)} %param.11, bf16[128,2048]{1,0:T(8,128)(2,1)} %param.12, f32[128,2048]{1,0:T(8,128)S(1)} %get-tuple-element.215, f32[128]{0:T(128)S(1)} %broadcast_multiply_fusion, f32[128]{0:T(128)S(1)} %get-tuple-element.212, f32[128]{0:T(128)S(1)} %get-tuple-element.213), kind=kLoop, calls=%fused_computation.27 | loop fusion | flops 2097152 | bytes 2622976 | tf_op jit(solution)/shard_map/convert_element_type | solution.py:447
  (9 shorter events, 0.1 us)
Async XLA Ops:
  0.6 11.6 %copy-start = (bf16[2048,32]{0,1:T(8,128)(2,1)S(1)}, bf16[2048,32]{0,1:T(8,128)(2,1)}, u32[]{:S(2)}) copy-start(bf16[2048,32]{0,1:T(8,128)(2,1)} %param.14) | copy-start | bytes 393220
  0.6 16.8 %copy-start.3 = (s32[4,2]{0,1:T(2,128)S(1)}, s32[4,2]{0,1:T(2,128)}, u32[]{:S(2)}) copy-start(s32[4,2]{0,1:T(2,128)} %param.17) | copy-start | bytes 100
  0.7 14.5 %copy-start.5 = (s32[128,1]{0,1:T(1,128)S(1)}, s32[128,1]{0,1:T(1,128)}, u32[]{:S(2)}) copy-start(s32[128,1]{0,1:T(1,128)} %param.18) | copy-start | bytes 1540
  0.7 16.8 %copy-start.1 = (bf16[8,256,768]{2,1,0:T(8,128)(2,1)S(1)}, bf16[8,256,768]{2,1,0:T(8,128)(2,1)}, u32[]{:S(2)}) copy-start(bf16[8,256,768]{2,1,0:T(8,128)(2,1)} %param.16) | copy-start | bytes 9437188
  14.0 0.8 copy-start.2
  17.4 120.2 %copy-start.4 = (f32[2048]{0:T(1024)S(1)}, f32[2048]{0:T(1024)}, u32[]{:S(2)}) copy-start(f32[2048]{0:T(1024)} %param.13) | copy-start | bytes 24580

commit v4 on v3

--- a/solution.py
+++ b/solution.py
@@ -333,7 +333,7 @@
     slice_ = 128
     parts = width // slice_
     vmem = pl.BlockSpec(memory_space=pltpu.VMEM)
-    any_ = pl.BlockSpec(memory_space=pl.ANY)
+    any_ = pl.BlockSpec(memory_space=pltpu.HBM)
     sent = 7 if ranks == 8 else ranks - 1
     bf16, f32 = jnp.bfloat16, jnp.float32
     return pl.pallas_call(
@@ -406,7 +406,7 @@
     grad_there = (mix_there[:, None] * grad_out).astype(jnp.bfloat16)
     plans = [()]
     if need_lists.shape[0] == 4:
-        plans = [((1, 2, 3), (2, 1, 0)), ((0, 2, 3), (2, 1, 0)), ()]
+        plans = [((1, 2, 3), (2, 1, 0)), ()]
     held = gate_up_weight.shape[0]
     good = [fits(need_lists, held, plan) for plan in plans]
     choice = jnp.int32(len(plans) - 1)

time: 142 us -> 132 us (0.930)
  other arithmetic: 12.6 us -> 8.07 us
  between operations: 8.42 us -> 5.92 us
    convert_element_type x1, other arithmetic: 2.24 us -> 0.23 us  [body(): grad_there = (mix_there[:, None] * grad_out).astype(jnp.bfloat16)]
where the time goes in v4:
time: 132 us
  Pallas kernels  115 us (87%)
  other arithmetic  8.07 us (6%)
  between operations  5.92 us (4%)
    pallas_call x1, Pallas kernels, experts(): pl.pallas_call(functools.partial(block_kernel, columns, ranks, relays), o...  115 us

profile of v4, /device:TPU:0, one launch (start us, length us, event | category | flops | bytes accessed | tf_op | source)
XLA Modules:
  0.0 131.6 jit_solution(11465828731142528523)
XLA Ops:
  0.6 0.0 copy-start
  0.6 0.0 copy-start.3
  0.7 0.0 copy-start.2
  0.7 0.0 copy-start.5
  0.7 1.3 fusion.3
  2.0 0.7 and_select_fusion
  2.7 1.7 %fusion.17 = (s32[]{:T(128)}, s32[]{:T(128)}, s32[]{:T(128)}, s32[]{:T(128)}, s32[2]{0:T(128)S(1)}) fusion(s32[4,2]{0,1:T(2,128)} %param.16, s32[4,2]{0,1:T(2,128)S(1)} %and_select_fusion, s32[]{:T(128)S(6)} %select_n.72), kind=kLoop, calls=%fused_computation.44 | loop fusion | flops 20 | bytes 100 | tf_op jit(solution)/shard_map/reduce_max | solution.py:375
  9.5 0.0 copy-done
  9.5 0.6 gather_fusion
  10.1 1.2 fusion.5
  11.3 0.3 fusion.25
  11.6 0.0 copy-done.5
  11.7 0.0 copy-done.2
  11.7 0.2 fusion.10
  11.9 0.0 copy-done.3
  12.0 0.0 copy-start.1
  12.0 0.0 copy-start.4
  12.0 116.2 %conditional.1 = ((bf16[128,2048]{1,0:T(8,128)(2,1)S(1)}, bf16[128,2048]{1,0:T(8,128)(2,1)S(1)}, bf16[128,2048]{1,0:T(8,128)(2,1)S(1)}, bf16[128,2048]{1,0:T(8,128)(2,1)S(1)})) conditional(s32[]{:T(128)} %clamp.3, (s32[4,2]{0,1:T(2,128)S(1)}, bf16[8,256,1536]{2,1,0:T(8,128)(2,1)}, bf16[8,256,768]{2,1,0:T(8,128)(2,1)}, ...), branch_computations={%region_5.6_spmd.clone, %region_6.7_spmd.clone} | conditional | bytes 72 | solution.py:415
  12.0 0.7 copy.18.need_ref
  12.7 115.3 %branch_0_fun.2 = (bf16[128,2048]{1,0:T(8,128)(2,1)S(1)}, bf16[128,2048]{1,0:T(8,128)(2,1)S(1)}, bf16[128,2048]{1,0:T(8,128)(2,1)S(1)}, bf16[128,2048]{1,0:T(8,128)(2,1)S(1)}) custom-call(s32[4,2]{1,0:T(4,128)} %copy.18.need_ref, bf16[8,256,1536]{2,1,0:T(8,128)(2,1)} %get-tuple-element.105.gate_up_ref, bf16[8,256,768]{2,1,0:T(8,128)(2,1)} %get-tuple-element.106.down_ref, ...), custom_call_target="tpu_custom_call" | custom-call | tf_op jit(solution)/shard_map/cond/branch_0_fun/pallas_call | solution.py:339
  128.2 0.0 copy-done.1
  128.2 1.6 %fusion.12 = (f32[128]{0:T(128)S(1)}, f32[128]{0:T(128)S(1)}, bf16[128,2048]{1,0:T(8,128)(2,1)}) fusion(bf16[128,2048]{1,0:T(8,128)(2,1)S(1)} %copy-done.2, bf16[128,2048]{1,0:T(8,128)(2,1)S(1)} %get-tuple-element.138, bf16[128,2048]{1,0:T(8,128)(2,1)S(1)} %get-tuple-element.139, f32[128]{0:T(128)S(1)} %get-tuple-element.152, f32[128]{0:T(128)S(1)} %get-tuple-element.153, ...), kind=kLoop, calls=%fused_computation.26 | loop fusion | flops 3407616 | bytes 2623488 | tf_op jit(solution)/shard_map/reduce_sum | solution.py:431
  129.8 0.0 copy-done.4
  129.8 0.5 fusion.8
  130.4 1.3 fusion.13
  (9 shorter events, 0.1 us)
Async XLA Ops:
  0.6 8.9 %copy-start = (bf16[2048,32]{0,1:T(8,128)(2,1)S(1)}, bf16[2048,32]{0,1:T(8,128)(2,1)}, u32[]{:S(2)}) copy-start(bf16[2048,32]{0,1:T(8,128)(2,1)} %param.13) | copy-start | bytes 393220
  0.6 11.3 %copy-start.3 = (s32[4,2]{0,1:T(2,128)S(1)}, s32[4,2]{0,1:T(2,128)}, u32[]{:S(2)}) copy-start(s32[4,2]{0,1:T(2,128)} %param.16) | copy-start | bytes 100
  0.7 11.0 %copy-start.2 = (bf16[128,2048]{1,0:T(8,128)(2,1)S(1)}, bf16[128,2048]{1,0:T(8,128)(2,1)}, u32[]{:S(2)}) copy-start(bf16[128,2048]{1,0:T(8,128)(2,1)} %param.11) | copy-start | bytes 1572868
  0.7 11.0 %copy-start.5 = (s32[128,1]{0,1:T(1,128)S(1)}, s32[128,1]{0,1:T(1,128)}, u32[]{:S(2)}) copy-start(s32[128,1]{0,1:T(1,128)} %param.17) | copy-start | bytes 1540
  12.0 116.2 %copy-start.1 = (bf16[128,2048]{1,0:T(8,128)(2,1)S(1)}, bf16[128,2048]{1,0:T(8,128)(2,1)}, u32[]{:S(2)}) copy-start(bf16[128,2048]{1,0:T(8,128)(2,1)} %param.10) | copy-start | bytes 1572868
  12.0 117.8 %copy-start.4 = (f32[2048]{0:T(1024)S(1)}, f32[2048]{0:T(1024)}, u32[]{:S(2)}) copy-start(f32[2048]{0:T(1024)} %param.12) | copy-start | bytes 24580
